TPU v7x, 32 devices: a whole 2x2x4 slice. The times are simulated.
32 devices in a mesh: groups: 2 (over y), ctx: 4 (over z), tp: 4 (over x, core).
Axes of the slice: x: 2, y: 2, z: 4, core: 2. Of those that a mesh axis runs over, the one named last changes fastest.
Arguments:
- queries: bfloat16 [64, 5120], P(('groups', 'ctx'), 'tp'), parts along dimension 0, may hold values from -12 to 12
- pool: bfloat16 [160, 2, 128, 1024], P(('groups', 'ctx'), None, None, 'tp'), parts along dimension 0, may hold values from -80 to 80
- resident: bfloat16 [4, 2, 512, 1024], P('groups', None, 'ctx', 'tp'), parts along dimension 0, may hold values from -6 to 6
- lengths: int32 [64], P(('groups', 'ctx')), parts along dimension 0, may hold values from 129 to 256
- table: int32 [64, 2], P(('groups', 'ctx')), parts along dimension 0, may hold values from 0 to 19, as said below
- moving_row_numbers: int32 [4], P('groups'), parts along dimension 0, may hold values from 0 to 31, as said below
- mover_table: int32 [4, 8], P('groups', 'ctx'), parts along dimension 0, may hold values from 0 to 19, as said below
- targets: int32 [4, 8], P('groups', 'ctx'), parts along dimension 0, may hold values from 0 to 3, as said below
Outputs:
- attended: bfloat16 [64, 5120], P(('groups', 'ctx'), 'tp'), parts along dimension 0
- received: bfloat16 [48, 2, 128, 1024], P(('groups', 'ctx'), None, None, 'tp'), parts along dimension 0
There are 2 independent parts, one for each index of `groups`. A program takes and returns all parts, laid end to end along the dimension named above; each array names one. Nothing has to cross between parts.
Inputs may be any that keep to these rules, and one draw needn't show every extreme that they name: On each ctx shard, the 8 x 2 entries of table for its rows and the 2 x 2 entries of mover_table in its columns name each of its 20 pages once. `mover_table`: see table. `moving_row_numbers`: distinct rows; the last row, 31, is always among them. `targets`: A page of shard c goes to one of the shards c, c + 1, ..., c + 2, counted mod 4. Every shard sends exactly 2 of its moving pages to one shard and at most 2 to any shard; some shard takes 2 pages from each of the 3 shards that may send to it.
All inputs are finite; a program needn't handle non-finite values.
Results may differ from a plain program's by a relative error of at most 0.0031.
Values may be sent and summed in bfloat16 or wider, within the bound.
A program may use at most 64 MiB of HBM per device.

v0:
```python
from functools import reduce
import math

import jax
import jax.numpy as jnp
from jax import lax
from jax.sharding import PartitionSpec as P

QUERY_HEADS = 40
KEY_VALUE_HEADS = 8
HEAD_SIZE = 128
PAGE_TOKENS = 128
RBLK = 2
REACH = 3
CAP = 2
ARRIVAL_SLOTS = 6


NEG_FILL = -1e30


def joined(part, axis, combine):
    gathered = jax.tree.map(lambda a: lax.all_gather(a, axis), part)

    def take(source):
        return jax.tree.map(lambda a: lax.dynamic_index_in_dim(a, source, 0, False), gathered)

    return lax.fori_loop(
        1, lax.axis_size(axis), lambda source, state: combine(state, take(source)), take(0)
    )


def from_behind(value, axis, steps):
    count = lax.axis_size(axis)
    pairs = [(source, (source + steps) % count) for source in range(count)]
    return lax.ppermute(value, axis, pairs)


def block_partial(query_per_row, key_rows, value_rows, live_mask):
    scale_factor = 1.0 / math.sqrt(HEAD_SIZE)
    scores = (
        jnp.einsum("rkgd,rtkd->rkgt", query_per_row, key_rows, preferred_element_type=jnp.float32)
        * scale_factor
    )
    live_wide = live_mask[:, None, None, :]
    scores = jnp.where(live_wide, scores, NEG_FILL)
    peak = jnp.max(scores, axis=-1)
    weight = jnp.where(live_wide, jnp.exp(scores - peak[..., None]), 0.0)
    total = jnp.sum(weight, axis=-1)
    block_sum = jnp.einsum(
        "rkgt,rtkd->rkgd",
        weight.astype(jnp.bfloat16),
        value_rows,
        preferred_element_type=jnp.float32,
    )
    return (peak, total, block_sum)


def combine(first, second):
    peak_first, total_first, acc_first = first
    peak_second, total_second, acc_second = second
    peak = jnp.maximum(peak_first, peak_second)
    scale_first = jnp.exp(peak_first - peak)
    scale_second = jnp.exp(peak_second - peak)
    total = total_first * scale_first + total_second * scale_second
    acc = acc_first * scale_first[..., None] + acc_second * scale_second[..., None]
    return (peak, total, acc)


def body(queries, pool, resident, lengths, table, moving_row_numbers, mover_table, targets):
    row_count = queries.shape[0]
    kv_width = pool.shape[3]
    local_heads = kv_width // HEAD_SIZE
    query_group_size = QUERY_HEADS // KEY_VALUE_HEADS
    shard_index = lax.axis_index("ctx")
    query_per_row = queries.reshape(row_count, local_heads, query_group_size, HEAD_SIZE)
    token_pos = jnp.arange(PAGE_TOKENS, dtype=jnp.int32)
    partials = []
    for block_index in range(RBLK):
        chosen = pool[table[:, block_index]]
        key_rows = chosen[:, 0].reshape(row_count, PAGE_TOKENS, local_heads, HEAD_SIZE)
        value_rows = chosen[:, 1].reshape(row_count, PAGE_TOKENS, local_heads, HEAD_SIZE)
        live_mask = block_index * PAGE_TOKENS + token_pos[None, :] < lengths[:, None]
        partials.append(block_partial(query_per_row, key_rows, value_rows, live_mask))
    row_peak, row_total, row_acc = reduce(combine, partials)
    mover_count = moving_row_numbers.shape[0]
    local_raw = moving_row_numbers - shard_index * row_count
    owned = (local_raw >= 0) & (local_raw < row_count)
    local_place = jnp.clip(local_raw, 0, row_count - 1)
    offered = jnp.where(owned[:, None], queries[local_place].astype(jnp.float32), 0.0)
    moving_query = lax.psum(offered, "ctx").astype(jnp.bfloat16)
    moving_query = moving_query.reshape(mover_count, local_heads, query_group_size, HEAD_SIZE)
    held_len = resident.shape[2]
    held_keys = resident[:, 0].reshape(mover_count, held_len, local_heads, HEAD_SIZE)
    held_values = resident[:, 1].reshape(mover_count, held_len, local_heads, HEAD_SIZE)
    live_all = jnp.ones((mover_count, held_len), dtype=bool)
    held_parts = [block_partial(moving_query, held_keys, held_values, live_all)]
    live_page = jnp.ones((mover_count, PAGE_TOKENS), dtype=bool)
    for block_index in range(mover_table.shape[1]):
        chosen = pool[mover_table[:, block_index]]
        key_rows = chosen[:, 0].reshape(mover_count, PAGE_TOKENS, local_heads, HEAD_SIZE)
        value_rows = chosen[:, 1].reshape(mover_count, PAGE_TOKENS, local_heads, HEAD_SIZE)
        held_parts.append(block_partial(moving_query, key_rows, value_rows, live_page))
    held_state = reduce(combine, held_parts)
    placed = (
        jnp.where(owned[:, None, None], row_peak[local_place], NEG_FILL),
        jnp.where(owned[:, None, None], row_total[local_place], 0.0),
        jnp.where(owned[:, None, None, None], row_acc[local_place], 0.0),
    )
    local_parts = combine(held_state, placed)
    merged = joined(local_parts, "ctx", combine)
    mover_out = merged[2] / merged[1][..., None]
    row_out = row_acc / row_total[..., None]
    match = (jnp.arange(row_count, dtype=jnp.int32)[:, None] == local_raw[None, :]) & owned[None, :]
    picked = jnp.sum(jnp.where(match[:, :, None, None, None], mover_out[None], 0.0), axis=1)
    row_out = jnp.where(jnp.any(match, axis=1)[:, None, None, None], picked, row_out)
    attended = row_out.reshape(row_count, local_heads * query_group_size * HEAD_SIZE).astype(
        jnp.bfloat16
    )
    page_count = targets.shape[0] * targets.shape[1]
    offsets = jnp.mod(targets.reshape(page_count) - shard_index, lax.axis_size("ctx"))
    order = jnp.arange(page_count, dtype=jnp.int32)
    earlier = order[None, :] < order[:, None]
    rank = jnp.sum(((offsets[None, :] == offsets[:, None]) & earlier).astype(jnp.int32), axis=1)
    slot = offsets * CAP + rank
    anchor = mover_table.reshape(page_count)
    slot_match = slot[None, :] == jnp.arange(ARRIVAL_SLOTS, dtype=jnp.int32)[:, None]
    chosen_page = jnp.sum(jnp.where(slot_match, anchor[None, :], 0), axis=1)
    filled = jnp.any(slot_match, axis=1)
    outgoing = jnp.where(
        filled[:, None, None, None], pool[chosen_page], jnp.zeros((), jnp.bfloat16)
    )
    outgoing = outgoing.reshape(REACH, CAP, 2, PAGE_TOKENS, kv_width)
    arrived = [outgoing[0]]
    for step_index in range(1, REACH):
        arrived.append(from_behind(outgoing[step_index], "ctx", step_index))
    received = jnp.concatenate(arrived, axis=0)
    return (attended, received)


def solution(mesh):
    in_specs = (
        P(("groups", "ctx"), "tp"),
        P(("groups", "ctx"), None, None, "tp"),
        P("groups", None, "ctx", "tp"),
        P(("groups", "ctx")),
        P(("groups", "ctx"), None),
        P("groups"),
        P("groups", "ctx"),
        P("groups", "ctx"),
    )
    out_specs = (P(("groups", "ctx"), "tp"), P(("groups", "ctx"), None, None, "tp"))
    return jax.shard_map(body, mesh=mesh, in_specs=in_specs, out_specs=out_specs, check_vma=False)
```

profile of v0, /device:TPU:0, one launch (start us, length us, event | category | flops | bytes accessed | tf_op | source)
XLA Modules:
  0.0 107.9 jit_solution(11978702353629267100)
XLA Ops:
  0.7 0.8 broadcast_subtract_fusion
  1.5 0.1 sub.230
  1.6 0.2 convert_reduce_fusion
  1.8 0.8 broadcast_in_dim.236
  2.6 0.1 fusion.52
  2.6 0.1 select_reduce_fusion.1
  2.8 0.6 gather_fusion.8
  3.4 0.1 broadcast_select_fusion
  3.5 0.8 fusion.69
  4.3 3.0 %collective-permute-start = (bf16[2,2,128,256]{3,2,1,0:T(8,128)(2,1)}, bf16[2,2,128,256]{3,2,1,0:T(8,128)(2,1)}, u32[]{:S(2)}, u32[]{:S(2)}) collective-permute-start(bf16[2,2,128,256]{3,2,1,0:T(8,128)(2,1)} %get-tuple-element.231), channel_id=1, source_target_pairs={{0,4},{4,8},{8,12},{12,0},{1,5},{5,9},{9,13},{13,1},{2,6},{6,10},{... | collective-permute-start | bytes 786440 | tf_op jit(solution)/shard_map/ppermute | solution.py:36
  7.4 2.6 %collective-permute-start.1 = (bf16[2,2,128,256]{3,2,1,0:T(8,128)(2,1)}, bf16[2,2,128,256]{3,2,1,0:T(8,128)(2,1)}, u32[]{:S(2)}, u32[]{:S(2)}) collective-permute-start(bf16[2,2,128,256]{3,2,1,0:T(8,128)(2,1)} %get-tuple-element.230), channel_id=1, source_target_pairs={{0,8},{4,12},{8,0},{12,4},{1,9},{5,13},{9,1},{13,5},{2,10},{6,14},... | collective-permute-start | bytes 786440 | tf_op jit(solution)/shard_map/ppermute | solution.py:36
  10.0 0.2 fusion.57
  10.2 1.6 %gather_fusion.3 = bf16[8,2,128,256]{3,2,1,0:T(8,128)(2,1)} fusion(bf16[20,2,128,256]{3,2,1,0:T(8,128)(2,1)S(1)} %copy-done, s32[1024]{0:T(1024)S(1)} %get-tuple-element.260), kind=kCustom, calls=%fused_computation.3 | custom fusion | bytes 2097184 | tf_op jit(solution)/shard_map/gather | solution.py:80
  11.8 2.3 %fusion.67 = (bf16[8,1,128,256]{3,2,1,0:T(8,128)(2,1)}, bf16[8,1,128,256]{3,2,1,0:T(8,128)(2,1)}) fusion(bf16[8,2,128,256]{3,2,1,0:T(8,128)(2,1)} %gather_fusion.3), kind=kLoop, calls=%fused_computation.146 | loop fusion | bytes 2097152 | tf_op jit(solution)/shard_map/slice | solution.py:82
  14.0 1.3 %copy.79 = bf16[8,1,128,256]{2,3,0,1:T(8,128)(2,1)S(1)} copy(bf16[8,1,128,256]{3,2,1,0:T(8,128)(2,1)} %get-tuple-element.226) | data formatting | bytes 1048576 | tf_op jit(solution)/shard_map/slice | solution.py:81
  15.4 1.6 %gather_fusion.4 = bf16[8,2,128,256]{3,2,1,0:T(8,128)(2,1)} fusion(bf16[20,2,128,256]{3,2,1,0:T(8,128)(2,1)S(1)} %copy-done, s32[1024]{0:T(1024)S(1)} %get-tuple-element.259), kind=kCustom, calls=%fused_computation.4 | custom fusion | bytes 2097184 | tf_op jit(solution)/shard_map/gather | solution.py:80
  17.0 2.3 %fusion.68 = (bf16[8,1,128,256]{3,2,1,0:T(8,128)(2,1)}, bf16[8,1,128,256]{3,2,1,0:T(8,128)(2,1)}) fusion(bf16[8,2,128,256]{3,2,1,0:T(8,128)(2,1)} %gather_fusion.4), kind=kLoop, calls=%fused_computation.147 | loop fusion | bytes 2097152 | tf_op jit(solution)/shard_map/slice | solution.py:82
  19.3 2.0 %copy.82 = bf16[8,1,128,256]{2,3,0,1:T(8,128)(2,1)} copy(bf16[8,1,128,256]{3,2,1,0:T(8,128)(2,1)} %get-tuple-element.228) | data formatting | bytes 1048576 | tf_op jit(solution)/shard_map/slice | solution.py:81
  21.3 2.1 %copy.93 = bf16[8,1,128,256]{2,3,0,1:T(8,128)(2,1)} copy(bf16[8,1,128,256]{3,2,1,0:T(8,128)(2,1)} %get-tuple-element.227) | data formatting | bytes 1048576 | tf_op jit(solution)/shard_map/slice | solution.py:82
  23.4 2.0 %copy.91 = bf16[8,1,128,256]{2,3,0,1:T(8,128)(2,1)} copy(bf16[8,1,128,256]{3,2,1,0:T(8,128)(2,1)} %get-tuple-element.225) | data formatting | bytes 1048576 | tf_op jit(solution)/shard_map/slice | solution.py:82
  25.6 0.6 gather_fusion
  26.1 0.3 fusion.74
  26.5 0.2 fusion.16
  26.7 1.4 %fusion.73 = (f32[8,2,5]{2,1,0:T(2,128)S(1)}, f32[8,2,5,128]{3,2,1,0:T(8,128)S(1)}) fusion(bf16[8,128,2,128]{1,3,2,0:T(8,128)(2,1)} %bitcast.150, bf16[8,2,5,128]{3,0,2,1:T(8,128)(2,1)S(1)} %bitcast.152, pred[8,128]{1,0:T(8,128)(4,1)S(1)} %get-tuple-element.248), kind=kOutput, calls=%fused_computation.152 | convolution fusion | flops 2652080 | bytes 587072 | tf_op jit(solution)/shard_map/rkgd,rtkd->rkgt/dot_general | solution.py:42
  28.0 0.2 fusion.18
  28.2 0.6 multiply_add_fusion
  28.8 1.5 %convolution_multiply_fusion = f32[8,2,5,128]{3,2,1,0:T(8,128)S(1)} fusion(bf16[8,128,2,128]{1,3,2,0:T(8,128)(2,1)} %bitcast.154, f32[8,2,5,128]{3,2,1,0:T(8,128)S(1)} %get-tuple-element.250, f32[8,2,5]{2,1,0:T(2,128)S(1)} %bitcast.170, f32[8,2,5]{2,1,0:T(2,128)S(1)} %get-tuple-element.249, pred[8,128]{1,0:T(8,128)(4,1)S(1)} %get-tuple-element.248), kind=kOutput, calls=%fused_computation.19 | convolution fusion | flops 2662400 | bytes 607872 | tf_op jit(solution)/shard_map/rkgt,rtkd->rkgd/dot_general | solution.py:50
  30.3 1.5 %fusion.8 = f32[8,2,5,128]{3,2,1,0:T(8,128)S(1)} fusion(f32[8,2,5,128]{3,2,1,0:T(8,128)S(1)} %convolution_multiply_fusion, bf16[8,128,2,128]{1,3,2,0:T(8,128)(2,1)} %bitcast.153, f32[8,2,5,128]{3,2,1,0:T(8,128)S(1)} %get-tuple-element.252, f32[8,2,5]{2,1,0:T(2,128)S(1)} %bitcast.169, f32[8,2,5]{2,1,0:T(2,128)S(1)} %get-tuple-element.251, ...), kind=kOutput, calls=%fused_computation.27 | convolution fusion | flops 2672640 | bytes 648832 | tf_op jit(solution)/shard_map/rkgt,rtkd->rkgd/dot_general | solution.py:50
  31.8 1.2 %gather_fusion.7 = f32[2,2,5,128]{3,2,1,0:T(8,128)} fusion(f32[8,2,5,128]{3,2,1,0:T(8,128)S(1)} %fusion.8, s32[1024]{0:T(1024)S(1)} %pad_clamp_fusion.5), kind=kCustom, calls=%fused_computation.7 | custom fusion | bytes 20488 | tf_op jit(solution)/shard_map/gather | solution.py:108
  32.9 1.1 %gather_fusion.5 = f32[2,2,5]{2,1,0:T(2,128)} fusion(f32[8,2,5]{2,1,0:T(2,128)S(1)} %bitcast.168, s32[1024]{0:T(1024)S(1)} %pad_clamp_fusion.5), kind=kCustom, calls=%fused_computation.5 | custom fusion | bytes 168 | tf_op jit(solution)/shard_map/gather | solution.py:106
  34.1 1.2 %fusion.66 = (pred[8]{0:T(512)(128)(4,1)}, pred[8,2]{0,1:T(4,128)(4,1)}) fusion(pred[2]{0:T(512)(128)(4,1)S(1)} %get-tuple-element.223, s32[2]{0:T(128)S(1)} %get-tuple-element.224), kind=kLoop, calls=%fused_computation.145 | loop fusion | flops 40 | bytes 34 | tf_op jit(solution)/shard_map/reduce_or | solution.py:116
  35.3 16.7 %psum.7 = bf16[2,1280]{1,0:T(2,128)(2,1)S(1)} all-reduce(f32[2,1280]{1,0:T(2,128)S(1)} %convert_select_fusion), channel_id=1, replica_groups=mesh['groups'=2,'ctx'=4,'tp'=4] {'ctx'}, use_global_device_ids=true, to_apply=%region_1.2 | all-reduce | flops 2560 | bytes 15360 | tf_op jit(solution)/shard_map/psum | solution.py:91
  52.1 0.6 gather_fusion.2
  52.7 0.1 copy.77
  52.8 0.6 gather_fusion.1
  53.4 0.7 fusion.71
  54.1 1.0 copy.75
  55.1 0.8 fusion.75
  55.9 0.7 fusion.76
  56.6 1.0 fusion.72
  57.6 0.1 copy.110
  57.7 0.2 fusion.77
  58.0 0.1 copy.111
  58.1 1.0 copy.87
  59.1 0.1 copy.89
  59.2 0.9 fusion.32
  60.1 0.9 fusion.34
  61.0 0.2 fusion.30
  61.2 0.7 fusion.41
  61.9 0.2 convolution_multiply_fusion.6
  62.1 0.9 fusion.13
  63.1 1.0 fusion.11
  64.1 13.1 %all-gather = f32[8,2,5,128]{3,1,2,0:T(2,128)S(1)} all-gather(f32[2,2,5,128]{3,1,2,0:T(2,128)S(1)} %copy.95), channel_id=2, replica_groups=mesh['groups'=2,'ctx'=4,'tp'=4] {'ctx'}, dimensions={0}, use_global_device_ids=true | all-gather | bytes 51200 | tf_op jit(solution)/shard_map/all_gather | solution.py:23
  77.2 1.4 %gather_fusion.6 = f32[2,2,5]{2,1,0:T(2,128)S(1)} fusion(f32[8,2,5]{2,1,0:T(2,128)} %bitcast.164, s32[1024]{0:T(1024)} %copy-done.4), kind=kCustom, calls=%fused_computation.6 | custom fusion | bytes 168 | tf_op jit(solution)/shard_map/gather | solution.py:107
  78.6 0.7 fusion.44
  79.4 11.9 %all_gather.15 = f32[4,2,2,5]{3,2,1,0:T(2,128)S(1)} all-gather(f32[1,2,2,5]{3,2,1,0:T(2,128)S(1)} %get-tuple-element.238), channel_id=1, replica_groups=mesh['groups'=2,'ctx'=4,'tp'=4] {'ctx'}, dimensions={0}, use_global_device_ids=true | all-gather | bytes 400 | tf_op jit(solution)/shard_map/all_gather | solution.py:23
  91.2 11.9 %all_gather.14 = f32[4,2,2,5]{3,2,1,0:T(2,128)S(1)} all-gather(f32[1,2,2,5]{3,2,1,0:T(2,128)S(1)} %get-tuple-element.239), channel_id=1, replica_groups=mesh['groups'=2,'ctx'=4,'tp'=4] {'ctx'}, dimensions={0}, use_global_device_ids=true | all-gather | bytes 400 | tf_op jit(solution)/shard_map/all_gather | solution.py:23
  103.1 0.4 while.19
  103.1 0.1 fusion.94
  103.4 0.1 fusion.94
  103.5 0.7 select_reduce_fusion
  104.3 0.9 fusion.14
  105.2 0.6 convert_element_type.38
  105.9 2.0 %pad_maximum_fusion = bf16[6,2,128,256]{3,2,1,0:T(8,128)(2,1)} fusion(bf16[2,2,128,256]{3,2,1,0:T(8,128)(2,1)} %collective-permute-done.1, bf16[2,2,128,256]{3,2,1,0:T(8,128)(2,1)} %collective-permute-done, bf16[2,2,128,256]{3,2,1,0:T(8,128)(2,1)S(1)} %get-tuple-element.229), kind=kLoop, calls=%fused_computation.39 | loop fusion | flops 786432 | bytes 1572864 | tf_op jit(solution)/shard_map/concatenate | solution.py:137
  (49 shorter events, 0.6 us)
Async XLA Ops:
  0.6 2.1 %copy-start = (bf16[20,2,128,256]{3,2,1,0:T(8,128)(2,1)S(1)}, bf16[20,2,128,256]{3,2,1,0:T(8,128)(2,1)}, u32[]{:S(2)}) copy-start(bf16[20,2,128,256]{3,2,1,0:T(8,128)(2,1)} %param.11) | copy-start | bytes 7864324
  0.6 9.3 %copy-start.5 = (s32[2,2]{1,0:T(2,128)S(1)}, s32[2,2]{1,0:T(2,128)}, u32[]{:S(2)}) copy-start(s32[2,2]{1,0:T(2,128)} %param.16) | copy-start | bytes 52
  0.7 9.5 %copy-start.6 = (s32[8,2]{0,1:T(2,128)S(1)}, s32[8,2]{0,1:T(2,128)}, u32[]{:S(2)}) copy-start(s32[8,2]{0,1:T(2,128)} %param.14) | copy-start | bytes 196
  4.3 101.5 %collective-permute-start = (bf16[2,2,128,256]{3,2,1,0:T(8,128)(2,1)}, bf16[2,2,128,256]{3,2,1,0:T(8,128)(2,1)}, u32[]{:S(2)}, u32[]{:S(2)}) collective-permute-start(bf16[2,2,128,256]{3,2,1,0:T(8,128)(2,1)} %get-tuple-element.231), channel_id=1, source_target_pairs={{0,4},{4,8},{8,12},{12,0},{1,5},{5,9},{9,13},{13,1},{2,6},{6,10},{... | collective-permute-start | bytes 786440 | tf_op jit(solution)/shard_map/ppermute | solution.py:36
  7.4 98.5 %collective-permute-start.1 = (bf16[2,2,128,256]{3,2,1,0:T(8,128)(2,1)}, bf16[2,2,128,256]{3,2,1,0:T(8,128)(2,1)}, u32[]{:S(2)}, u32[]{:S(2)}) collective-permute-start(bf16[2,2,128,256]{3,2,1,0:T(8,128)(2,1)} %get-tuple-element.230), channel_id=1, source_target_pairs={{0,8},{4,12},{8,0},{12,4},{1,9},{5,13},{9,1},{13,5},{2,10},{6,14},... | collective-permute-start | bytes 786440 | tf_op jit(solution)/shard_map/ppermute | solution.py:36
  17.0 8.5 %copy-start.7 = (s32[2]{0:T(128)S(1)}, s32[2]{0:T(128)}, u32[]{:S(2)}) copy-start(s32[2]{0:T(128)} %param.15) | copy-start | bytes 28
  17.0 8.5 %copy-start.8 = (s32[8]{0:T(128)S(1)}, s32[8]{0:T(128)}, u32[]{:S(2)}) copy-start(s32[8]{0:T(128)} %param.13) | copy-start | bytes 100
  17.0 8.6 %copy-start.1 = (bf16[8,1280]{1,0:T(8,128)(2,1)S(1)}, bf16[8,1280]{1,0:T(8,128)(2,1)}, u32[]{:S(2)}) copy-start(bf16[8,1280]{1,0:T(8,128)(2,1)} %param.10) | copy-start | bytes 61444
  25.4 26.6 %copy-start.3 = (pred[2]{0:T(512)(128)(4,1)}, pred[2]{0:T(512)(128)(4,1)S(1)}, u32[]{:S(2)}) copy-start(pred[2]{0:T(512)(128)(4,1)S(1)} %get-tuple-element.223) | copy-start | bytes 10
  25.5 26.6 %copy-start.4 = (s32[1024]{0:T(1024)}, s32[1024]{0:T(1024)S(1)}, u32[]{:S(2)}) copy-start(s32[1024]{0:T(1024)S(1)} %pad_clamp_fusion.5) | copy-start | bytes 12292
  31.8 20.3 %copy-start.2 = (f32[8,2,5,128]{3,2,1,0:T(8,128)}, f32[8,2,5,128]{3,2,1,0:T(8,128)S(1)}, u32[]{:S(2)}) copy-start(f32[8,2,5,128]{3,2,1,0:T(8,128)S(1)} %fusion.8) | copy-start | bytes 122884
where the time goes:
time: 109 us; the launch traced here: 108 us
  blocking collectives  53.6 us (49%)
  local copies, waits for them, and re-layouts  27.9 us (26%)
  other arithmetic  11.4 us (10%)
  matrix products  8.49 us (8%)
  starting transfers between devices  5.61 us (5%)
    all_gather x3, blocking collectives, joined(): gathered = jax.tree.map(lambda a: lax.all_gather(a, axis), part)  36.9 us
    psum x1, blocking collectives, body(): moving_query = lax.psum(offered, 'ctx').astype(jnp.bfloat16)  16.7 us
    slice x4, local copies, waits for them, and re-layouts, body(): chosen[:, 1].reshape(row_count, PAGE_TOKENS, local_heads, HEAD_SIZE)  8.67 us
    ppermute x2, starting transfers between devices, from_behind(): return lax.ppermute(value, axis, pairs)  5.61 us
    dot_general x5, matrix products, block_partial(): jnp.einsum('rkgt,rtkd->rkgd', weight.astype(jnp.bfloat16), value_rows, pr...  5.06 us
    dot_general x5, matrix products, block_partial(): jnp.einsum('rkgd,rtkd->rkgt', query_per_row, key_rows, preferred_element_...  3.43 us
    slice x2, local copies, waits for them, and re-layouts, body(): chosen[:, 0].reshape(row_count, PAGE_TOKENS, local_heads, HEAD_SIZE)  3.35 us
    gather x2, local copies, waits for them, and re-layouts, body(): chosen = pool[table[:, block_index]]  3.21 us
  transfers between devices with their start and end apart: 2, of which 0 were waited for; matrix products, arithmetic and copies ran while one was open for 39% of the time, Pallas kernels for 0%

commit v1 on v0

v1 whole, which is shorter than its diff:
```python
import functools
import math

import jax
import jax.numpy as jnp
from jax import lax
from jax.experimental import pallas as pl
from jax.experimental.pallas import tpu as pltpu
from jax.sharding import PartitionSpec as P

QUERY_HEADS = 40
KEY_VALUE_HEADS = 8
HEAD_SIZE = 128
PAGE_TOKENS = 128
REACH = 3
CAP = 2
ARRIVAL_SLOTS = 6
HEAD_ROWS = 16
POOL_PIECES = 4

NEG_FILL = -1e30
MESH = pl.DeviceIdType.MESH


def block_partial(query, keys, values, live):
    scores = lax.dot_general(
        query, keys, (((1,), (1,)), ((), ())), preferred_element_type=jnp.float32
    ) * (1.0 / math.sqrt(HEAD_SIZE))
    if live is not None:
        scores = jnp.where(live, scores, NEG_FILL)
    peak = jnp.max(scores, axis=1, keepdims=True)
    weight = jnp.exp(scores - peak)
    if live is not None:
        weight = jnp.where(live, weight, 0.0)
    total = jnp.sum(weight, axis=1, keepdims=True)
    acc = jnp.dot(weight.astype(jnp.bfloat16), values, preferred_element_type=jnp.float32)
    return peak, total, acc


def combine(first, second):
    peak = jnp.maximum(first[0], second[0])
    scale_first = jnp.exp(first[0] - peak)
    scale_second = jnp.exp(second[0] - peak)
    return (
        peak,
        first[1] * scale_first + second[1] * scale_second,
        first[2] * scale_first + second[2] * scale_second,
    )


def kernel(
    n, group,
    lengths, table, moving, mover_table, targets, q_ref, pool_hbm, resident_hbm,
    attended, received,
    pool, resident, stage, heads, asked, parts, result,
    pool_sem, resident_sem, keep_sem, page_send, page_recv, ask_send, ask_recv, part_send, part_recv,
):
    rows = q_ref.shape[0]
    head_count = q_ref.shape[1] // HEAD_SIZE
    pages = pool_hbm.shape[0]
    movers = moving.shape[0]
    me = lax.axis_index("ctx")

    def peer_at(step):
        return lax.rem(me + step, n)

    def each_peer(act):
        if n <= 8:
            for step in range(1, n):
                act(step)
        else:
            pl.loop(1, n)(act)

    piece = pages // POOL_PIECES
    fetches = [
        pltpu.make_async_copy(
            pool_hbm.at[pl.ds(i * piece, piece)], pool.at[pl.ds(i * piece, piece)], pool_sem.at[i]
        )
        for i in range(POOL_PIECES)
    ]
    fetch_resident = pltpu.make_async_copy(resident_hbm, resident, resident_sem)
    for fetch in fetches:
        fetch.start()
    fetch_resident.start()

    barrier = pltpu.get_barrier_semaphore()

    def greet(step):
        pl.semaphore_signal(barrier, inc=1, device_id={"ctx": peer_at(step)}, device_id_type=MESH)

    each_peer(greet)

    heads[...] = jnp.zeros_like(heads)
    for h in range(head_count):
        heads[:, h, :] = q_ref[:, h * HEAD_SIZE : (h + 1) * HEAD_SIZE].astype(jnp.float32)
    pool[pages] = jnp.zeros(pool.shape[1:], pool.dtype)
    for g in range(movers):
        place = jnp.clip(moving[g] - me * rows, 0, rows - 1)
        asked[me, g] = heads[place].astype(jnp.bfloat16)

    pl.semaphore_wait(barrier, n - 1)

    def ask(step):
        return pltpu.make_async_remote_copy(
            src_ref=asked.at[me], dst_ref=asked.at[me],
            send_sem=ask_send.at[step], recv_sem=ask_recv.at[step],
            device_id={"ctx": peer_at(step)}, device_id_type=MESH,
        )

    each_peer(lambda step: ask(step).start())

    named = [(g, b) for g in range(movers) for b in range(mover_table.shape[1])]
    offsets = [lax.rem(targets[g, b] - me + n, n) for g, b in named]
    slots = []
    for i, offset in enumerate(offsets):
        rank = jnp.int32(0)
        for before in offsets[:i]:
            rank = rank + jnp.where(before == offset, 1, 0)
        slots.append(offset * CAP + rank)

    def page_of(slot):
        page = jnp.int32(pages)
        for (g, b), taken in zip(named, slots):
            page = jnp.where(taken == slot, mover_table[g, b], page)
        return page

    def page_copy(offset, rank):
        slot = offset * CAP + rank
        return pltpu.make_async_remote_copy(
            src_ref=stage.at[slot], dst_ref=received.at[slot],
            send_sem=page_send.at[slot], recv_sem=page_recv.at[slot],
            device_id={"ctx": peer_at(offset)}, device_id_type=MESH,
        )

    for fetch in fetches:
        fetch.wait()
    page_copies = []
    for offset in range(REACH - 1, 0, -1):
        for rank in range(CAP):
            slot = offset * CAP + rank
            stage[slot] = pool[page_of(slot)]
            copy = page_copy(offset, rank)
            copy.start()
            page_copies.append(copy)
    for slot in range(CAP):
        stage[slot] = pool[page_of(slot)]
    keep = pltpu.make_async_copy(
        stage.at[pl.ds(0, CAP)], received.at[pl.ds(0, CAP)], keep_sem
    )
    keep.start()

    head = lax.broadcasted_iota(jnp.int32, (HEAD_ROWS, HEAD_SIZE), 0)
    token = lax.broadcasted_iota(jnp.int32, (HEAD_ROWS, PAGE_TOKENS), 1)
    upper = head < group

    def spread(query):
        query = query.astype(jnp.float32)
        return jnp.concatenate(
            [jnp.where(upper, query, 0.0), jnp.where(upper, 0.0, query)], axis=1
        ).astype(jnp.bfloat16)

    def own_half(state):
        peak, total, acc = state
        return peak, total, jnp.where(upper, acc[:, :HEAD_SIZE], acc[:, HEAD_SIZE:])

    states = []
    for row in range(rows):
        query = spread(heads[row])
        blocks = []
        for b in range(table.shape[1]):
            page = table[row, b]
            live = b * PAGE_TOKENS + token < lengths[row]
            blocks.append(block_partial(query, pool[page, 0], pool[page, 1], live))
        states.append(own_half(functools.reduce(combine, blocks)))

    fetch_resident.wait()
    each_peer(lambda step: ask(step).wait_recv())
    lane = lax.broadcasted_iota(jnp.int32, (HEAD_ROWS, HEAD_SIZE), 1)
    for g in range(movers):
        owner = lax.div(moving[g], jnp.int32(rows))
        query = spread(asked[owner, g])
        blocks = [block_partial(query, resident[g, 0], resident[g, 1], None)]
        for b in range(mover_table.shape[1]):
            page = mover_table[g, b]
            blocks.append(block_partial(query, pool[page, 0], pool[page, 1], None))
        peak, total, acc = own_half(functools.reduce(combine, blocks))
        parts[me, g, 0] = acc
        parts[me, g, 1] = jnp.where(lane < HEAD_SIZE // 2, peak, total)

    def tell(step):
        return pltpu.make_async_remote_copy(
            src_ref=parts.at[me], dst_ref=parts.at[me],
            send_sem=part_send.at[step], recv_sem=part_recv.at[step],
            device_id={"ctx": peer_at(step)}, device_id_type=MESH,
        )

    each_peer(lambda step: tell(step).start())
    each_peer(lambda step: tell(step).wait_recv())

    def part_of(source, g):
        stats = parts[source, g, 1]
        return stats[:, :1], stats[:, HEAD_SIZE // 2 : HEAD_SIZE // 2 + 1], parts[source, g, 0]

    merged = []
    for g in range(movers):
        if n <= 8:
            merged.append(functools.reduce(combine, [part_of(e, g) for e in range(n)]))
        else:
            merged.append(
                lax.fori_loop(
                    1, n, lambda e, state, g=g: combine(state, part_of(e, g)), part_of(0, g)
                )
            )
    for row in range(rows):
        peak, total, acc = (
            jnp.full((HEAD_ROWS, 1), NEG_FILL, jnp.float32),
            jnp.zeros((HEAD_ROWS, 1), jnp.float32),
            jnp.zeros((HEAD_ROWS, HEAD_SIZE), jnp.float32),
        )
        for g in range(movers):
            here = moving[g] - me * rows - row
            narrow = jnp.broadcast_to(here, (HEAD_ROWS, 1)) == 0
            wide = jnp.broadcast_to(here, (HEAD_ROWS, HEAD_SIZE)) == 0
            peak = jnp.where(narrow, merged[g][0], peak)
            total = jnp.where(narrow, merged[g][1], total)
            acc = jnp.where(wide, merged[g][2], acc)
        peak, total, acc = combine(states[row], (peak, total, acc))
        result[row] = acc / total
    for h in range(head_count):
        attended[:, h * HEAD_SIZE : (h + 1) * HEAD_SIZE] = result[:, h, :].astype(attended.dtype)

    each_peer(lambda step: ask(step).wait_send())
    each_peer(lambda step: tell(step).wait_send())
    keep.wait()
    for copy in page_copies:
        copy.wait()


def body(queries, pool, resident, lengths, table, moving_row_numbers, mover_table, targets):
    n = lax.axis_size("ctx")
    rows, width = queries.shape
    pages = pool.shape[0]
    movers = moving_row_numbers.shape[0]
    smem = pl.BlockSpec(memory_space=pltpu.SMEM)
    vmem = pl.BlockSpec(memory_space=pltpu.VMEM)
    anywhere = pl.BlockSpec(memory_space=pl.ANY)
    page_shape = pool.shape[1:]
    return pl.pallas_call(
        functools.partial(kernel, n, QUERY_HEADS // KEY_VALUE_HEADS),
        out_shape=(
            jax.ShapeDtypeStruct((rows, width), jnp.bfloat16),
            jax.ShapeDtypeStruct((ARRIVAL_SLOTS,) + page_shape, jnp.bfloat16),
        ),
        in_specs=[smem] * 5 + [vmem, anywhere, anywhere],
        out_specs=(vmem, anywhere),
        scratch_shapes=[
            pltpu.VMEM((pages + 1,) + page_shape, jnp.bfloat16),
            pltpu.VMEM(resident.shape, jnp.bfloat16),
            pltpu.VMEM((ARRIVAL_SLOTS,) + page_shape, jnp.bfloat16),
            pltpu.VMEM((rows, HEAD_ROWS, HEAD_SIZE), jnp.float32),
            pltpu.VMEM((n, movers, HEAD_ROWS, HEAD_SIZE), jnp.bfloat16),
            pltpu.VMEM((n, movers, 2, HEAD_ROWS, HEAD_SIZE), jnp.float32),
            pltpu.VMEM((rows, HEAD_ROWS, HEAD_SIZE), jnp.float32),
            pltpu.SemaphoreType.DMA((POOL_PIECES,)),
            pltpu.SemaphoreType.DMA,
            pltpu.SemaphoreType.DMA,
            pltpu.SemaphoreType.DMA((ARRIVAL_SLOTS,)),
            pltpu.SemaphoreType.DMA((ARRIVAL_SLOTS,)),
            pltpu.SemaphoreType.DMA((n,)),
            pltpu.SemaphoreType.DMA((n,)),
            pltpu.SemaphoreType.DMA((n,)),
            pltpu.SemaphoreType.DMA((n,)),
        ],
        compiler_params=pltpu.CompilerParams(
            collective_id=0, has_side_effects=True, vmem_limit_bytes=32 * 1024 * 1024
        ),
    )(lengths, table, moving_row_numbers, mover_table, targets, queries, pool, resident)


def solution(mesh):
    in_specs = (
        P(("groups", "ctx"), "tp"),
        P(("groups", "ctx"), None, None, "tp"),
        P("groups", None, "ctx", "tp"),
        P(("groups", "ctx")),
        P(("groups", "ctx"), None),
        P("groups"),
        P("groups", "ctx"),
        P("groups", "ctx"),
    )
    out_specs = (P(("groups", "ctx"), "tp"), P(("groups", "ctx"), None, None, "tp"))
    return jax.shard_map(body, mesh=mesh, in_specs=in_specs, out_specs=out_specs, check_vma=False)
```

time: 109 us -> 37.7 us (0.35)
  blocking collectives: 53.6 us -> 0 us
  Pallas kernels: 0 us -> 28.4 us
  local copies, waits for them, and re-layouts: 27.9 us -> 8.32 us
  other arithmetic: 11.4 us -> 0 us
  matrix products: 8.49 us -> 0 us
  starting transfers between devices: 5.61 us -> 0 us
    all_gather x3 -> x0, blocking collectives: 36.9 us -> none  [joined(): gathered = jax.tree.map(lambda a: lax.all_gather(a, axis), part)]
    pallas_call x0 -> x1, Pallas kernels: none -> 28.4 us  [body(): pl.pallas_call(functools.partial(kernel, n, QUERY_HEADS // KEY_VALUE_HEAD...]
    slice x14 -> x0, local copies, waits for them, and re-layouts: 16.9 us -> none  [the longest x4 8.67 us: body(): chosen[:, 1].reshape(row_count, PAGE_TOKENS, local_heads, HEAD_SIZE)]
    psum x1 -> x0, blocking collectives: 16.7 us -> none  [body(): moving_query = lax.psum(offered, 'ctx').astype(jnp.bfloat16)]
    gather x9 -> x0, local copies, waits for them, and re-layouts: 9.17 us -> none  [the longest x2 3.21 us: body(): chosen = pool[table[:, block_index]]]
    dot_general x10 -> x0, matrix products: 8.49 us -> none  [the longest x5 5.06 us: block_partial(): jnp.einsum('rkgt,rtkd->rkgd', weight.astype(jnp.bfloat16), value_rows, pr...]
    unnamed x20 -> x17, local copies, waits for them, and re-layouts: 0.29 us -> 8.32 us
    ppermute x2 -> x0, starting transfers between devices: 5.61 us -> none  [from_behind(): return lax.ppermute(value, axis, pairs)]
  transfers between devices with their start and end apart: 2 -> 0, of which waited for: 0 -> 0; matrix products, arithmetic and copies ran while one was open for 39% -> 0% of each run, Pallas kernels for 0% -> 0%
where the time goes in v1:
time: 37.7 us; the launch traced here: 37.4 us
  Pallas kernels  28.4 us (75%)
  local copies, waits for them, and re-layouts  8.32 us (22%)
  between operations  0.65 us (2%)
    pallas_call x1, Pallas kernels, body(): pl.pallas_call(functools.partial(kernel, n, QUERY_HEADS // KEY_VALUE_HEAD...  28.4 us
    unnamed x17, local copies, waits for them, and re-layouts  8.32 us

profile of v1, /device:TPU:0, one launch (start us, length us, event | category | flops | bytes accessed | tf_op | source)
XLA Modules:
  0.0 37.4 jit_solution(3197451888321609768)
XLA Ops:
  0.6 0.8 %copy.10.table = s32[8,2]{1,0:T(8,128)S(1)} copy(s32[8,2]{0,1:T(2,128)} %param.12) | data formatting | bytes 128 | tf_op args[4]
  1.4 0.0 copy-start
  1.4 1.7 %copy-done = bf16[20,2,128,256]{3,2,1,0:T(8,128)(2,1)S(1)} copy-done((bf16[20,2,128,256]{3,2,1,0:T(8,128)(2,1)S(1)}, bf16[20,2,128,256]{3,2,1,0:T(8,128)(2,1)}, u32[]{:S(2)}) %copy-start) | copy-done | bytes 2621464
  3.1 0.0 copy-start.1
  3.1 0.9 %copy-done.1 = bf16[2,2,128,256]{3,2,1,0:T(8,128)(2,1)S(1)} copy-done((bf16[2,2,128,256]{3,2,1,0:T(8,128)(2,1)S(1)}, bf16[2,2,128,256]{3,2,1,0:T(8,128)(2,1)}, u32[]{:S(2)}) %copy-start.1) | copy-done | bytes 262168
  4.1 0.0 copy-start.2
  4.1 0.7 %copy-done.2 = bf16[8,1280]{1,0:T(8,128)(2,1)S(1)} copy-done((bf16[8,1280]{1,0:T(8,128)(2,1)S(1)}, bf16[8,1280]{1,0:T(8,128)(2,1)}, u32[]{:S(2)}) %copy-start.2) | copy-done | bytes 20504
  4.8 0.0 copy-start.3
  4.8 0.7 %copy-done.3 = s32[2,2]{1,0:T(2,128)S(1)} copy-done((s32[2,2]{1,0:T(2,128)S(1)}, s32[2,2]{1,0:T(2,128)}, u32[]{:S(2)}) %copy-start.3) | copy-done | bytes 40
  5.5 0.0 copy-start.4
  5.5 0.7 %copy-done.4 = s32[2,2]{1,0:T(2,128)S(1)} copy-done((s32[2,2]{1,0:T(2,128)S(1)}, s32[2,2]{1,0:T(2,128)}, u32[]{:S(2)}) %copy-start.4) | copy-done | bytes 40
  6.2 0.0 copy-start.5
  6.2 0.7 %copy-done.5 = s32[8]{0:T(128)S(1)} copy-done((s32[8]{0:T(128)S(1)}, s32[8]{0:T(128)}, u32[]{:S(2)}) %copy-start.5) | copy-done | bytes 56
  6.8 0.0 copy-start.6
  6.8 0.7 %copy-done.6 = s32[2]{0:T(128)S(1)} copy-done((s32[2]{0:T(128)S(1)}, s32[2]{0:T(128)}, u32[]{:S(2)}) %copy-start.6) | copy-done | bytes 32
  7.5 28.4 %shard_map.95 = (bf16[8,1280]{1,0:T(8,128)(2,1)S(1)}, bf16[6,2,128,256]{3,2,1,0:T(8,128)(2,1)S(1)}) custom-call(s32[8]{0:T(128)S(1)} %copy-done.5, s32[8,2]{1,0:T(8,128)S(1)} %copy.10.table, s32[2]{0:T(128)S(1)} %copy-done.6, s32[2,2]{1,0:T(2,128)S(1)} %copy-done.3, s32[2,2]{1,0:T(2,128)S(1)} %copy-done.4, bf16[8,1280]{1,0:T(8,128)(2,1)S(1)} %copy-done.2, ...), custom_call_target="tpu_custom_call" | custom-call | tf_op jit(solution)/shard_map/pallas_call | solution.py:248
  35.9 0.6 %copy.13 = bf16[8,1280]{1,0:T(8,128)(2,1)} copy(bf16[8,1280]{1,0:T(8,128)(2,1)S(1)} %get-tuple-element.4) | data formatting | bytes 40960
  36.5 0.9 %copy.14 = bf16[6,2,128,256]{3,2,1,0:T(8,128)(2,1)} copy(bf16[6,2,128,256]{3,2,1,0:T(8,128)(2,1)S(1)} %get-tuple-element.5) | data formatting | bytes 1572864
Async XLA Ops:
  1.4 1.7 %copy-start = (bf16[20,2,128,256]{3,2,1,0:T(8,128)(2,1)S(1)}, bf16[20,2,128,256]{3,2,1,0:T(8,128)(2,1)}, u32[]{:S(2)}) copy-start(bf16[20,2,128,256]{3,2,1,0:T(8,128)(2,1)} %pool_hbm.1) | copy-start | bytes 7864324
  3.1 0.9 %copy-start.1 = (bf16[2,2,128,256]{3,2,1,0:T(8,128)(2,1)S(1)}, bf16[2,2,128,256]{3,2,1,0:T(8,128)(2,1)}, u32[]{:S(2)}) copy-start(bf16[2,2,128,256]{3,2,1,0:T(8,128)(2,1)} %resident_hbm.1) | copy-start | bytes 786436
  4.1 0.7 %copy-start.2 = (bf16[8,1280]{1,0:T(8,128)(2,1)S(1)}, bf16[8,1280]{1,0:T(8,128)(2,1)}, u32[]{:S(2)}) copy-start(bf16[8,1280]{1,0:T(8,128)(2,1)} %q_ref.1) | copy-start | bytes 61444
  4.8 0.7 %copy-start.3 = (s32[2,2]{1,0:T(2,128)S(1)}, s32[2,2]{1,0:T(2,128)}, u32[]{:S(2)}) copy-start(s32[2,2]{1,0:T(2,128)} %mover_table.1) | copy-start | bytes 52
  5.5 0.7 %copy-start.4 = (s32[2,2]{1,0:T(2,128)S(1)}, s32[2,2]{1,0:T(2,128)}, u32[]{:S(2)}) copy-start(s32[2,2]{1,0:T(2,128)} %targets.1) | copy-start | bytes 52
  6.2 0.7 %copy-start.5 = (s32[8]{0:T(128)S(1)}, s32[8]{0:T(128)}, u32[]{:S(2)}) copy-start(s32[8]{0:T(128)} %lengths.1) | copy-start | bytes 100
  6.8 0.7 %copy-start.6 = (s32[2]{0:T(128)S(1)}, s32[2]{0:T(128)}, u32[]{:S(2)}) copy-start(s32[2]{0:T(128)} %moving.1) | copy-start | bytes 28

commit v2 on v1

--- a/solution.py
+++ b/solution.py
@@ -17,15 +17,18 @@
 ARRIVAL_SLOTS = 6
 HEAD_ROWS = 16
 POOL_PIECES = 4
+VMEM_BYTES = 60 * 1024 * 1024
 
 NEG_FILL = -1e30
 MESH = pl.DeviceIdType.MESH
 
 
-def block_partial(query, keys, values, live):
-    scores = lax.dot_general(
-        query, keys, (((1,), (1,)), ((), ())), preferred_element_type=jnp.float32
-    ) * (1.0 / math.sqrt(HEAD_SIZE))
+def block_partials(queries, keys, values, live, own_half):
+    scores = [
+        lax.dot_general(q, k, (((1,), (1,)), ((), ())), preferred_element_type=jnp.float32)
+        for q, k in zip(queries, keys)
+    ]
+    scores = jnp.concatenate(scores, axis=0) * (1.0 / math.sqrt(HEAD_SIZE))
     if live is not None:
         scores = jnp.where(live, scores, NEG_FILL)
     peak = jnp.max(scores, axis=1, keepdims=True)
@@ -33,8 +36,23 @@
     if live is not None:
         weight = jnp.where(live, weight, 0.0)
     total = jnp.sum(weight, axis=1, keepdims=True)
-    acc = jnp.dot(weight.astype(jnp.bfloat16), values, preferred_element_type=jnp.float32)
-    return peak, total, acc
+    weight = weight.astype(jnp.bfloat16)
+    sums = [
+        own_half(
+            jnp.dot(
+                weight[i * HEAD_ROWS : (i + 1) * HEAD_ROWS], v, preferred_element_type=jnp.float32
+            )
+        )
+        for i, v in enumerate(values)
+    ]
+    return peak, total, jnp.concatenate(sums, axis=0)
+
+
+def joined(state, count):
+    size = state[0].shape[0] // count
+    return functools.reduce(
+        combine, [tuple(a[i * size : (i + 1) * size] for a in state) for i in range(count)]
+    )
 
 
 def combine(first, second):
@@ -159,33 +177,28 @@
             [jnp.where(upper, query, 0.0), jnp.where(upper, 0.0, query)], axis=1
         ).astype(jnp.bfloat16)
 
-    def own_half(state):
-        peak, total, acc = state
-        return peak, total, jnp.where(upper, acc[:, :HEAD_SIZE], acc[:, HEAD_SIZE:])
-
-    states = []
-    for row in range(rows):
-        query = spread(heads[row])
-        blocks = []
-        for b in range(table.shape[1]):
-            page = table[row, b]
-            live = b * PAGE_TOKENS + token < lengths[row]
-            blocks.append(block_partial(query, pool[page, 0], pool[page, 1], live))
-        states.append(own_half(functools.reduce(combine, blocks)))
+    def own_half(acc):
+        return jnp.where(upper, acc[:, :HEAD_SIZE], acc[:, HEAD_SIZE:])
 
     fetch_resident.wait()
     each_peer(lambda step: ask(step).wait_recv())
     lane = lax.broadcasted_iota(jnp.int32, (HEAD_ROWS, HEAD_SIZE), 1)
+    owners = [lax.div(moving[g], jnp.int32(rows)) for g in range(movers)]
+    queries = [spread(asked[owners[g], g]) for g in range(movers)]
+    held = mover_table.shape[1] + 1
+    keys = [resident[g, 0] for g in range(movers)]
+    values = [resident[g, 1] for g in range(movers)]
+    for b in range(held - 1):
+        for g in range(movers):
+            keys.append(pool[mover_table[g, b], 0])
+            values.append(pool[mover_table[g, b], 1])
+    state = joined(block_partials(queries * held, keys, values, None, own_half), held)
     for g in range(movers):
-        owner = lax.div(moving[g], jnp.int32(rows))
-        query = spread(asked[owner, g])
-        blocks = [block_partial(query, resident[g, 0], resident[g, 1], None)]
-        for b in range(mover_table.shape[1]):
-            page = mover_table[g, b]
-            blocks.append(block_partial(query, pool[page, 0], pool[page, 1], None))
-        peak, total, acc = own_half(functools.reduce(combine, blocks))
-        parts[me, g, 0] = acc
-        parts[me, g, 1] = jnp.where(lane < HEAD_SIZE // 2, peak, total)
+        peak, total, acc = (a[g * HEAD_ROWS : (g + 1) * HEAD_ROWS] for a in state)
+        parts[me, g * head_count : (g + 1) * head_count] = acc[:head_count]
+        for i, column in enumerate((peak, total)):
+            at = movers * head_count + 2 * g + i
+            parts[me, at : at + 1] = jnp.sum(jnp.where(lane == head, column, 0.0), axis=0, keepdims=True)
 
     def tell(step):
         return pltpu.make_async_remote_copy(
@@ -195,11 +208,28 @@
         )
 
     each_peer(lambda step: tell(step).start())
+
+    queries = [spread(heads[row]) for row in range(rows)]
+    own_blocks = table.shape[0]
+    places = [(b, row) for b in range(own_blocks) for row in range(rows)]
+    keys = [pool[table[b, row], 0] for b, row in places]
+    values = [pool[table[b, row], 1] for b, row in places]
+    live = jnp.concatenate(
+        [b * PAGE_TOKENS + token < lengths[row] for b, row in places], axis=0
+    )
+    state = joined(block_partials(queries * own_blocks, keys, values, live, own_half), own_blocks)
+
     each_peer(lambda step: tell(step).wait_recv())
 
     def part_of(source, g):
-        stats = parts[source, g, 1]
-        return stats[:, :1], stats[:, HEAD_SIZE // 2 : HEAD_SIZE // 2 + 1], parts[source, g, 0]
+        at = movers * head_count + 2 * g
+        peak, total = (
+            jnp.sum(jnp.where(lane == head, parts[source, i : i + 1], 0.0), axis=1, keepdims=True)
+            for i in (at, at + 1)
+        )
+        acc = parts[source, g * head_count : (g + 1) * head_count]
+        padding = jnp.zeros((HEAD_ROWS - head_count, HEAD_SIZE), jnp.float32)
+        return peak, total, jnp.concatenate([acc, padding], axis=0)
 
     merged = []
     for g in range(movers):
@@ -211,21 +241,25 @@
                     1, n, lambda e, state, g=g: combine(state, part_of(e, g)), part_of(0, g)
                 )
             )
-    for row in range(rows):
-        peak, total, acc = (
-            jnp.full((HEAD_ROWS, 1), NEG_FILL, jnp.float32),
-            jnp.zeros((HEAD_ROWS, 1), jnp.float32),
-            jnp.zeros((HEAD_ROWS, HEAD_SIZE), jnp.float32),
-        )
-        for g in range(movers):
-            here = moving[g] - me * rows - row
-            narrow = jnp.broadcast_to(here, (HEAD_ROWS, 1)) == 0
-            wide = jnp.broadcast_to(here, (HEAD_ROWS, HEAD_SIZE)) == 0
-            peak = jnp.where(narrow, merged[g][0], peak)
-            total = jnp.where(narrow, merged[g][1], total)
-            acc = jnp.where(wide, merged[g][2], acc)
-        peak, total, acc = combine(states[row], (peak, total, acc))
-        result[row] = acc / total
+    def row_of(width):
+        return lax.div(lax.broadcasted_iota(jnp.int32, (rows * HEAD_ROWS, width), 0), HEAD_ROWS)
+
+    def down(part):
+        return jnp.concatenate([part] * rows, axis=0)
+
+    extra = (
+        jnp.full((rows * HEAD_ROWS, 1), NEG_FILL, jnp.float32),
+        jnp.zeros((rows * HEAD_ROWS, 1), jnp.float32),
+        jnp.zeros((rows * HEAD_ROWS, HEAD_SIZE), jnp.float32),
+    )
+    for g in range(movers):
+        place = moving[g] - me * rows
+        extra = tuple(
+            jnp.where(row_of(old.shape[1]) == place, down(new), old)
+            for new, old in zip(merged[g], extra)
+        )
+    peak, total, acc = combine(state, extra)
+    result[...] = (acc / total).reshape(result.shape)
     for h in range(head_count):
         attended[:, h * HEAD_SIZE : (h + 1) * HEAD_SIZE] = result[:, h, :].astype(attended.dtype)
 
@@ -245,6 +279,7 @@
     vmem = pl.BlockSpec(memory_space=pltpu.VMEM)
     anywhere = pl.BlockSpec(memory_space=pl.ANY)
     page_shape = pool.shape[1:]
+    part_rows = -(-movers * (width // HEAD_SIZE + 2) // 8) * 8
     return pl.pallas_call(
         functools.partial(kernel, n, QUERY_HEADS // KEY_VALUE_HEADS),
         out_shape=(
@@ -259,7 +294,7 @@
             pltpu.VMEM((ARRIVAL_SLOTS,) + page_shape, jnp.bfloat16),
             pltpu.VMEM((rows, HEAD_ROWS, HEAD_SIZE), jnp.float32),
             pltpu.VMEM((n, movers, HEAD_ROWS, HEAD_SIZE), jnp.bfloat16),
-            pltpu.VMEM((n, movers, 2, HEAD_ROWS, HEAD_SIZE), jnp.float32),
+            pltpu.VMEM((n, part_rows, HEAD_SIZE), jnp.float32),
             pltpu.VMEM((rows, HEAD_ROWS, HEAD_SIZE), jnp.float32),
             pltpu.SemaphoreType.DMA((POOL_PIECES,)),
             pltpu.SemaphoreType.DMA,
@@ -272,9 +307,9 @@
             pltpu.SemaphoreType.DMA((n,)),
         ],
         compiler_params=pltpu.CompilerParams(
-            collective_id=0, has_side_effects=True, vmem_limit_bytes=32 * 1024 * 1024
+            collective_id=0, has_side_effects=True, vmem_limit_bytes=VMEM_BYTES
         ),
-    )(lengths, table, moving_row_numbers, mover_table, targets, queries, pool, resident)
+    )(lengths, table.T, moving_row_numbers, mover_table, targets, queries, pool, resident)
 
 
 def solution(mesh):

time: 37.7 us -> 30.8 us (0.82)
  local copies, waits for them, and re-layouts: 8.32 us -> 3.4 us
  Pallas kernels: 28.4 us -> 26.5 us
    unnamed x17 -> x2, local copies, waits for them, and re-layouts: 8.32 us -> 3.4 us
    pallas_call x1, Pallas kernels: 28.4 us -> 26.5 us  [body(): pl.pallas_call(functools.partial(kernel, n, QUERY_HEADS // KEY_VALUE_HEAD...]
where the time goes in v2:
time: 30.8 us; the launch traced here: 30.6 us
  Pallas kernels  26.5 us (86%)
  local copies, waits for them, and re-layouts  3.4 us (11%)
  between operations  0.64 us (2%)
    pallas_call x1, Pallas kernels, body(): pl.pallas_call(functools.partial(kernel, n, QUERY_HEADS // KEY_VALUE_HEAD...  26.5 us
    unnamed x2, local copies, waits for them, and re-layouts  3.4 us

profile of v2, /device:TPU:0, one launch (start us, length us, event | category | flops | bytes accessed | tf_op | source)
XLA Modules:
  0.0 30.6 jit_solution(11268101218893810005)
XLA Ops:
  0.6 26.5 %shard_map.95 = (bf16[8,1280]{1,0:T(8,128)(2,1)}, bf16[6,2,128,256]{3,2,1,0:T(8,128)(2,1)}) custom-call(s32[8]{0:T(128)} %lengths.1, s32[2,8]{1,0:T(2,128)} %bitcast.1, s32[2]{0:T(128)} %moving.1, s32[2,2]{1,0:T(2,128)} %mover_table.1, s32[2,2]{1,0:T(2,128)} %targets.1, bf16[8,1280]{1,0:T(8,128)(2,1)} %q_ref.1, bf16[20,2,128,256]{3,2,1,0:T(8,128)(2,1)} %pool_hbm.1, ...), custom_call_target="tpu_custom_call" | custom-call | tf_op jit(solution)/shard_map/pallas_call | solution.py:283
  27.2 1.3 %copy.12 = bf16[8,1280]{1,0:T(8,128)(2,1)} copy(bf16[8,1280]{1,0:T(8,128)(2,1)} %get-tuple-element.4) | data formatting | bytes 40960
  28.5 2.1 %copy.13 = bf16[6,2,128,256]{3,2,1,0:T(8,128)(2,1)} copy(bf16[6,2,128,256]{3,2,1,0:T(8,128)(2,1)} %get-tuple-element.5) | data formatting | bytes 1572864
